TPU v7x, 32 devices: a whole 2x2x4 slice. The times are simulated.
32 devices in a mesh: group: 2 (over y), blk: 8 (over z, x), layer: 2 (over core).
Axes of the slice: x: 2, y: 2, z: 4, core: 2. Of those that a mesh axis runs over, the one named last changes fastest.
Arguments:
- query_grads: bfloat16 [4096, 4, 4096], P(('group', 'blk'), 'layer'), parts along dimension 0, may hold values from -6 to 6
- train_grads: bfloat16 [64, 4, 4096], P(('group', 'blk'), 'layer'), parts along dimension 0, may hold values from -6 to 6
- basis_in: float32 [4, 64, 64], P('layer'), may hold values from -0.75 to 0.75
- basis_out: float32 [4, 64, 64], P('layer'), may hold values from -0.75 to 0.75
- eigen_in: float32 [4, 64], P('layer'), may hold values from 0.3 to 3
- eigen_out: float32 [4, 64], P('layer'), may hold values from 0.3 to 3
Outputs:
- influence: float32 [4096, 32], P(('group', 'blk'), 'layer'), parts along dimension 0
There are 2 independent parts, one for each index of `group`. A program takes and returns all parts, laid end to end along the dimension named above; an argument that names none is the same for every part. Nothing has to cross between parts.
All inputs are finite; a program needn't handle non-finite values.
Results may differ from a plain program's by a relative error of at most 0.0029.
Values may be sent and summed in bfloat16 or wider, within the bound.
A program may use at most 128 MiB of HBM per device.

v0:
```python
import jax
import jax.numpy as jnp
from jax import lax
from jax.sharding import PartitionSpec as P

RA = 64
RB = 64


def shards(query_grads, train_grads, basis_in, basis_out, eigen_in, eigen_out):
    q_rows, layer_count, width = query_grads.shape
    t_rows = train_grads.shape[0]
    mats = query_grads.astype(jnp.float32).reshape(q_rows, layer_count, RA, RB)
    coef = jnp.einsum(
        "lia,qlib,lbj->qlaj", basis_in, mats, basis_out, precision=lax.Precision.HIGHEST
    )
    denom = eigen_in[:, :, None] * eigen_out[:, None, :] + 0.1
    scaled = coef / denom[None]
    back = jnp.einsum(
        "lia,qlaj,lbj->qlib", basis_in, scaled, basis_out, precision=lax.Precision.HIGHEST
    )
    precond = back.reshape(q_rows, layer_count * width).astype(jnp.bfloat16)
    train_flat = train_grads.reshape(t_rows, layer_count * width)
    all_layers = layer_count * lax.axis_size("layer")
    factor = 1.0 / jnp.sqrt(jnp.float32(all_layers * width))
    partial_value = lax.dot_general(
        precond,
        lax.all_gather(train_flat, "blk", axis=0, tiled=True),
        (((1,), (1,)), ((), ())),
        preferred_element_type=jnp.float32,
    )
    return lax.psum_scatter(partial_value * factor, "layer", scatter_dimension=1, tiled=True)


def solution(mesh):
    placed = (
        P(("group", "blk"), "layer", None),
        P(("group", "blk"), "layer", None),
        P("layer", None, None),
        P("layer", None, None),
        P("layer", None),
        P("layer", None),
    )
    return jax.shard_map(
        shards, mesh=mesh, in_specs=placed, out_specs=P(("group", "blk"), "layer"), check_vma=False
    )
```

profile of v0, /device:TPU:0, one launch (start us, length us, event | category | flops | bytes accessed | tf_op | source)
XLA Modules:
  0.0 117.7 jit_solution(24784395260393411)
XLA Ops:
  6.5 0.0 copy-start
  6.5 0.0 reduce-scatter.2.cloned.1.call-start
  6.5 11.1 %copy.8 = bf16[256,2,4096]{0,2,1:T(8,128)(2,1)} copy(bf16[256,2,4096]{2,1,0:T(2,128)(2,1)} %param.6) | data formatting | bytes 8388608 | tf_op args[0]
  17.6 0.0 copy-start.3
  17.6 0.0 copy-start.4
  17.6 0.0 copy-start.1
  17.6 0.0 copy-done
  17.6 8.4 %fusion.11 = f32[256,2,64,64]{0,3,2,1:T(8,128)S(1)} fusion(bf16[256,2,64,64]{0,3,2,1:T(8,128)(2,1)} %bitcast.33, f32[2,64,64]{2,1,0:T(8,128)S(1)} %copy-done), kind=kOutput, calls=%fused_computation.10 | convolution fusion | flops 1610612736 | bytes 12615680 | tf_op jit(solution)/shard_map/lia,qlib,lbj->qlaj/dot_general | solution.py:14
  26.0 0.0 copy-done.3
  26.0 0.0 copy-done.4
  26.0 0.1 multiply_add_fusion
  26.1 0.0 copy-done.1
  26.1 13.0 %divide_bitcast_fusion = f32[256,2,64,64]{0,3,2,1:T(8,128)S(1)} fusion(f32[2,64,64]{2,1,0:T(8,128)S(1)} %multiply_add_fusion, f32[256,2,64,64]{0,3,2,1:T(8,128)S(1)} %fusion.11, f32[2,64,64]{2,1,0:T(8,128)S(1)} %copy-done.1), kind=kOutput, calls=%fused_computation.6 | convolution fusion | flops 1612709888 | bytes 16842752 | tf_op jit(solution)/shard_map/lia,qlib,lbj->qlaj/dot_general | solution.py:14
  39.2 13.6 %fusion.8 = f32[256,2,64,64]{0,3,2,1:T(8,128)S(1)} fusion(f32[256,2,64,64]{0,3,2,1:T(8,128)S(1)} %divide_bitcast_fusion, f32[2,64,64]{2,1,0:T(8,128)S(1)} %copy-done), kind=kOutput, calls=%fused_computation.9 | convolution fusion | flops 1610612736 | bytes 16809984 | tf_op jit(solution)/shard_map/lia,qlaj,lbj->qlib/dot_general | solution.py:19
  52.8 0.0 copy-start.2
  52.8 12.5 %fusion.16 = bf16[2,256,64,64]{1,3,2,0:T(8,128)(2,1)} fusion(f32[256,2,64,64]{0,3,2,1:T(8,128)S(1)} %fusion.8, f32[2,64,64]{2,1,0:T(8,128)S(1)} %copy-done.1), kind=kOutput, calls=%fused_computation.11 | convolution fusion | flops 1612709888 | bytes 12615680 | tf_op jit(solution)/shard_map/lia,qlaj,lbj->qlib/dot_general | solution.py:19
  65.4 0.0 copy-done.2
  65.4 33.0 %all-gather = bf16[8,4,8192]{2,1,0:T(4,128)(2,1)S(1)} all-gather(bf16[1,4,8192]{2,1,0:T(4,128)(2,1)S(1)} %reshape.14), channel_id=1, replica_groups=mesh['group'=2,'blk'=8,'layer'=2] {'blk'}, dimensions={0}, use_global_device_ids=true | all-gather | bytes 589824 | tf_op jit(solution)/shard_map/all_gather | solution.py:28
  98.4 0.1 reshape.15
  98.6 3.6 %convolution_multiply_fusion = f32[256,32]{0,1:T(8,128)} fusion(bf16[32,8192]{1,0:T(8,128)(2,1)S(1)} %reshape.15, bf16[256,8192]{0,1:T(8,128)(2,1)} %bitcast.32), kind=kOutput, calls=%fused_computation.12 | convolution fusion | flops 134225920 | bytes 4751360 | tf_op jit(solution)/shard_map/dot_general | solution.py:26
  102.2 0.0 reduce-scatter.2.cloned.1.call-update
  102.2 8.7 %reduce-scatter.2.cloned.1.call-done = f32[256,16]{0,1:T(8,128)} async-done(((f32[256,32]{0,1:T(8,128)}), f32[256,16]{0,1:T(8,128)}) %reduce-scatter.2.cloned.1.call-update) | async-done | bytes 16400 | tf_op jit(solution)/shard_map/reduce_scatter | solution.py:32
  (1 shorter events, 0.0 us)
Async XLA Ops:
  6.5 11.1 %copy-start = (f32[2,64,64]{2,1,0:T(8,128)S(1)}, f32[2,64,64]{2,1,0:T(8,128)}, u32[]{:S(2)}) copy-start(f32[2,64,64]{2,1,0:T(8,128)} %param.8) | copy-start | bytes 98308
  6.5 104.3 %reduce-scatter.2.cloned.1.call-start = ((), (), s32[]{:S(2)}) async-start(), calls=%async_computation.1 | async-start | bytes 49152 | tf_op jit(solution)/shard_map/reduce_scatter | solution.py:32
  17.6 8.4 %copy-start.3 = (f32[2,64]{1,0:T(2,128)S(1)}, f32[2,64]{1,0:T(2,128)}, u32[]{:S(2)}) copy-start(f32[2,64]{1,0:T(2,128)} %param.11) | copy-start | bytes 1540
  17.6 8.4 %copy-start.4 = (f32[2,64]{1,0:T(2,128)S(1)}, f32[2,64]{1,0:T(2,128)}, u32[]{:S(2)}) copy-start(f32[2,64]{1,0:T(2,128)} %param.10) | copy-start | bytes 1540
  17.6 8.5 %copy-start.1 = (f32[2,64,64]{2,1,0:T(8,128)S(1)}, f32[2,64,64]{2,1,0:T(8,128)}, u32[]{:S(2)}) copy-start(f32[2,64,64]{2,1,0:T(8,128)} %param.9) | copy-start | bytes 98308
  52.8 12.6 %copy-start.2 = (bf16[4,2,4096]{2,1,0:T(2,128)(2,1)S(1)}, bf16[4,2,4096]{2,1,0:T(2,128)(2,1)}, u32[]{:S(2)}) copy-start(bf16[4,2,4096]{2,1,0:T(2,128)(2,1)} %param.7) | copy-start | bytes 196612
Sparse Core Ops, SparseCore 0:
  102.3 8.5 reduce-scatter.1
where the time goes:
time: 118 us
  matrix products  51.2 us (43%)
  blocking collectives  33 us (28%)
  between operations  13.5 us (11%)
  local copies, waits for them, and re-layouts  11.3 us (10%)
  waiting for transfers between devices  8.7 us (7%)
    all_gather x1, blocking collectives, shards(): lax.all_gather(train_flat, 'blk', axis=0, tiled=True)  33 us
    dot_general x2, matrix products, shards(): jnp.einsum('lia,qlaj,lbj->qlib', basis_in, scaled, basis_out, precision=l...  26.2 us
    dot_general x2, matrix products, shards(): jnp.einsum('lia,qlib,lbj->qlaj', basis_in, mats, basis_out, precision=lax...  21.4 us
    unnamed x13, local copies, waits for them, and re-layouts  11.3 us
    reduce_scatter x1, waiting for transfers between devices, shards(): lax.psum_scatter(partial_value * factor, 'layer', scatter_dimension=1, ti...  8.68 us
    dot_general x1, matrix products, shards(): lax.dot_general(precond, lax.all_gather(train_flat, 'blk', axis=0, tiled=...  3.61 us
  transfers between devices with their start and end apart: 1, of which 1 were waited for; matrix products, arithmetic and copies ran while one was open for 0% of the time, Pallas kernels for 0%

commit v1 on v0

v1 whole, which is shorter than its diff:
```python
import jax
import jax.numpy as jnp
from jax import lax
from jax.experimental import pallas as pl
from jax.experimental.pallas import tpu as pltpu
from jax.sharding import PartitionSpec as P

RA = 64
RB = 64
MESH = pl.DeviceIdType.MESH
F32 = jnp.float32
BF16 = jnp.bfloat16


def split(x):
    high = x.astype(BF16)
    return high, (x - high.astype(F32)).astype(BF16)


def dot(a, b, dims):
    return lax.dot_general(a, b, (dims, ((), ())), preferred_element_type=F32)


def dot_wide(a, b, dims):
    ah, al = split(a)
    bh, bl = split(b)
    return dot(ah, bh, dims) + (dot(ah, bl, dims) + dot(al, bh, dims))


def kernel(n, scale, q_hbm, t_hbm, a_ref, b_ref, ei_ref, eo_ref, out_ref,
           qv, tv, wide, narrow, basis_pad, blocks, prod, part, other,
           q_sem, t_sem, send_sem, recv_sem, x_send, x_recv):
    group = lax.axis_index("group")
    me = lax.axis_index("blk")
    layer = lax.axis_index("layer")
    chunks = qv.shape[0]
    q_rows = qv.shape[1]
    t_rows = tv.shape[1]
    half = chunks // 2
    last = n // 2

    def block_at(pos):
        pos = lax.rem(pos + 2 * n, n)
        return jnp.where(pos < last, 2 * pos, 2 * (n - 1 - pos) + 1)

    pos = jnp.where(lax.rem(me, 2) == 0, me // 2, n - 1 - me // 2)
    right = (group, block_at(pos + 1), layer)
    left = (group, block_at(pos - 1), layer)
    partner = (group, me, 1 - layer)

    barrier = pltpu.get_barrier_semaphore()
    for device in (right, left, partner):
        pl.semaphore_signal(barrier, inc=1, device_id=device, device_id_type=MESH)

    def t_copy(c):
        return pltpu.make_async_copy(
            t_hbm.at[:, :, pl.ds(pl.multiple_of(c * 128, 128), 128)], tv.at[c], t_sem.at[c])

    def q_copy(c):
        return pltpu.make_async_copy(
            q_hbm.at[:, :, pl.ds(pl.multiple_of(c * 128, 128), 128)], qv.at[c], q_sem.at[c])

    @pl.loop(0, chunks)
    def _(c):
        t_copy(c).start()

    @pl.loop(0, chunks)
    def _(c):
        q_copy(c).start()

    b0, b1 = b_ref[0], b_ref[1]
    both = jnp.concatenate([b0, b1], axis=1)
    zero = jnp.zeros((RB, 128), F32)
    right_mat = jnp.concatenate(
        [jnp.concatenate([both, zero], axis=1), jnp.concatenate([zero, both], axis=1)], axis=0)

    @pl.loop(0, chunks)
    def _(c):
        t_copy(c).wait()

    rows = chunks * t_rows * 2
    t_all = tv[...].reshape(rows, 128)
    rh, rl = split(right_mat)
    turned = dot(t_all, rh, ((1,), (0,))) + dot(t_all, rl, ((1,), (0,)))
    for h in range(2):
        wide[h] = turned[:, h * 128:(h + 1) * 128]
    for l in range(2):
        basis_pad[l] = jnp.concatenate([a_ref[l], jnp.zeros((RA, 128 - RA), F32)], axis=1)

    eye = lax.broadcasted_iota(jnp.int32, (RA, RA), 0) == lax.broadcasted_iota(jnp.int32, (RA, RA), 1)
    step = 2 * t_rows
    for l in range(2):
        basis = jnp.concatenate(
            [basis_pad[l, pl.ds(h, RA // 2, stride=2), :] for h in range(2)], axis=0)[:, :RA]
        pieces = []
        for h in range(2):
            pieces.append(jnp.concatenate(
                [wide[h, pl.ds(2 * t + l, chunks, stride=step), :][:, l * 64:l * 64 + 64]
                 for t in range(t_rows)], axis=1))
        moved = jnp.concatenate(pieces, axis=0)
        coef = dot_wide(basis, moved, ((0,), (0,)))
        e_in = jnp.sum(jnp.where(eye, jnp.broadcast_to(ei_ref[l:l + 1, :], (RA, RA)), 0.0), axis=1, keepdims=True)
        denom = e_in * eo_ref[l:l + 1, :] + 0.1
        scaled = coef / jnp.concatenate([denom] * t_rows, axis=1)
        back = dot_wide(basis, scaled, ((1,), (0,)))
        for t in range(t_rows):
            narrow[pl.ds(2 * t + l, chunks, stride=step), :] = jnp.concatenate(
                [back[h * 32:(h + 1) * 32, t * 64:(t + 1) * 64] for h in range(2)], axis=1)

    zero_b = jnp.zeros((RB, RB), F32)
    left_mat = jnp.concatenate(
        [jnp.concatenate([b0, zero_b], axis=1), jnp.concatenate([zero_b, b0], axis=1),
         jnp.concatenate([b1, zero_b], axis=1), jnp.concatenate([zero_b, b1], axis=1)], axis=0)
    final = dot_wide(narrow[...], left_mat, ((1,), (1,)))
    parity = lax.rem(lax.broadcasted_iota(jnp.int32, (rows, 128), 0), 2)
    mine = jnp.where(parity == 0, final[:, :128], final[:, 128:])
    blocks[me] = mine.reshape(chunks, step, 128).astype(BF16)

    pl.semaphore_wait(barrier, 3)

    def hop(flow, d, side):
        owner = block_at(pos - d + 1 if flow == 0 else pos + d - 1)
        piece = blocks.at[owner, pl.ds(side * half, half)]
        return pltpu.make_async_remote_copy(
            src_ref=piece, dst_ref=piece,
            send_sem=send_sem.at[flow, d - 1, side], recv_sem=recv_sem.at[flow, d - 1, side],
            device_id=right if flow == 0 else left, device_id_type=MESH)

    def arrival(flow, d, side):
        owner = block_at(pos - d if flow == 0 else pos + d)
        piece = blocks.at[owner, pl.ds(side * half, half)]
        return pltpu.make_async_remote_copy(
            src_ref=piece, dst_ref=piece,
            send_sem=send_sem.at[flow, d - 1, side], recv_sem=recv_sem.at[flow, d - 1, side],
            device_id=right if flow == 0 else left, device_id_type=MESH)

    for side in range(2):
        for flow in range(2):
            hop(flow, 1, (side + flow) % 2).start()

    @pl.loop(1, last - 1)
    def _(d):
        for side in range(2):
            for flow in range(2):
                arrival(flow, d, (side + flow) % 2).wait_recv()
                hop(flow, d + 1, (side + flow) % 2).start()

    for flow in range(2):
        arrival(flow, last - 1, flow).wait_recv()
        hop(flow, last, flow).start()
    for flow in range(2):
        arrival(flow, last - 1, 1 - flow).wait_recv()

    @pl.loop(0, chunks)
    def _(c):
        q_copy(c).wait()

    for flow in range(2):
        arrival(flow, last, flow).wait_recv()

    total = None
    for c in range(0, chunks, 2):
        lhs = jnp.concatenate([qv[c + i].reshape(2 * q_rows, 128) for i in range(2)], axis=1)
        rhs = jnp.concatenate(
            [blocks[:, c + i].astype(F32).reshape(n * step, 128).astype(BF16) for i in range(2)], axis=1)
        term = dot(lhs, rhs, ((1,), (1,)))
        total = term if total is None else total + term
    columns = n * step
    tiles = prod.shape[0]
    if columns < tiles * 128:
        total = jnp.concatenate([total, jnp.zeros((2 * q_rows, tiles * 128 - columns), F32)], axis=1)
    for i in range(tiles):
        prod[i] = total[:, i * 128:(i + 1) * 128]

    def layer_rows(l):
        return jnp.concatenate(
            [prod[i, pl.ds(l, q_rows, stride=2), :].T for i in range(tiles)], axis=0)[:columns]

    first, second = layer_rows(0), layer_rows(1)
    odd = lax.rem(lax.broadcasted_iota(jnp.int32, (n * step, q_rows), 0), 2)
    prod_t = jnp.where(odd == 0, first, second)
    part_all = prod_t.reshape(n * t_rows, 2, q_rows).sum(axis=1) * scale
    part[...] = part_all.reshape(part.shape)

    swap = pltpu.make_async_remote_copy(
        src_ref=part.at[1 - layer], dst_ref=other, send_sem=x_send, recv_sem=x_recv,
        device_id=partner, device_id_type=MESH)
    swap.start()

    @pl.loop(1, last)
    def _(d):
        for side in range(2):
            for flow in range(2):
                hop(flow, d, side).wait_send()
    for flow in range(2):
        hop(flow, last, flow).wait_send()
    swap.wait()
    out_ref[...] = part[layer] + other[...]


def solution(mesh):
    n = mesh.shape["blk"]

    def shards(q, t, a, b, ei, eo):
        q_rows, _, width = q.shape
        t_rows = t.shape[0]
        chunks = width // 128
        scale = 1.0 / float((2 * mesh.shape["layer"] * width) ** 0.5)
        keep = n * t_rows // 2
        rows = chunks * t_rows * 2
        vmem = pl.BlockSpec(memory_space=pltpu.VMEM)
        hbm = pl.BlockSpec(memory_space=pl.ANY)
        out = pl.pallas_call(
            lambda *refs: kernel(n, scale, *refs),
            out_shape=jax.ShapeDtypeStruct((keep, q_rows), F32),
            in_specs=[hbm, hbm, vmem, vmem, vmem, vmem],
            out_specs=vmem,
            scratch_shapes=[
                pltpu.VMEM((chunks, q_rows, 2, 128), BF16),
                pltpu.VMEM((chunks, t_rows, 2, 128), BF16),
                pltpu.VMEM((2, rows, 128), F32),
                pltpu.VMEM((rows, 128), F32),
                pltpu.VMEM((2, RA, 128), F32),
                pltpu.VMEM((n, chunks, 2 * t_rows, 128), BF16),
                pltpu.VMEM((-(-n * t_rows * 2 // 128), 2 * q_rows, 128), F32),
                pltpu.VMEM((2, keep, q_rows), F32),
                pltpu.VMEM((keep, q_rows), F32),
                pltpu.SemaphoreType.DMA((chunks,)),
                pltpu.SemaphoreType.DMA((chunks,)),
                pltpu.SemaphoreType.DMA((2, n // 2, 2)),
                pltpu.SemaphoreType.DMA((2, n // 2, 2)),
                pltpu.SemaphoreType.DMA,
                pltpu.SemaphoreType.DMA,
            ],
            compiler_params=pltpu.CompilerParams(
                collective_id=0, has_side_effects=True, vmem_limit_bytes=56 * 2**20),
        )(q, t, a, b, ei, eo)
        return out.T

    placed = (
        P(("group", "blk"), "layer", None),
        P(("group", "blk"), "layer", None),
        P("layer", None, None),
        P("layer", None, None),
        P("layer", None),
        P("layer", None),
    )
    return jax.shard_map(
        shards, mesh=mesh, in_specs=placed, out_specs=P(("group", "blk"), "layer"), check_vma=False
    )
```

time: 118 us -> 24.7 us (0.21)
  matrix products: 51.2 us -> 0 us
  blocking collectives: 33 us -> 0 us
  Pallas kernels: 0 us -> 23.2 us
  between operations: 13.5 us -> 0.01 us
  local copies, waits for them, and re-layouts: 11.3 us -> 1.32 us
  waiting for transfers between devices: 8.7 us -> 0 us
    dot_general x5 -> x0, matrix products: 51.2 us -> none  [the longest x2 26.2 us: shards(): jnp.einsum('lia,qlaj,lbj->qlib', basis_in, scaled, basis_out, precision=l...]
    all_gather x1 -> x0, blocking collectives: 33 us -> none  [shards(): lax.all_gather(train_flat, 'blk', axis=0, tiled=True)]
    pallas_call x0 -> x1, Pallas kernels: none -> 23.2 us  [shards(): pl.pallas_call(lambda *refs: kernel(n, scale, *refs), out_shape=jax.Shape...]
    unnamed x13 -> x1, local copies, waits for them, and re-layouts: 11.3 us -> 1.32 us
    reduce_scatter x1 -> x0, waiting for transfers between devices: 8.68 us -> none  [shards(): lax.psum_scatter(partial_value * factor, 'layer', scatter_dimension=1, ti...]
  transfers between devices with their start and end apart: 1 -> 0, of which waited for: 1 -> 0; matrix products, arithmetic and copies ran while one was open for 0% -> 0% of each run, Pallas kernels for 0% -> 0%
where the time goes in v1:
time: 24.7 us; the launch traced here: 24.5 us
  Pallas kernels  23.2 us (94%)
  local copies, waits for them, and re-layouts  1.32 us (5%)
    pallas_call x1, Pallas kernels, shards(): pl.pallas_call(lambda *refs: kernel(n, scale, *refs), out_shape=jax.Shape...  23.2 us
    unnamed x1, local copies, waits for them, and re-layouts  1.32 us

profile of v1, /device:TPU:0, one launch (start us, length us, event | category | flops | bytes accessed | tf_op | source)
XLA Modules:
  0.0 24.5 jit_solution(17342361885820018341)
XLA Ops:
  0.0 23.2 %shard_map.64 = f32[16,256]{1,0:T(8,128)} custom-call(bf16[256,2,4096]{2,1,0:T(2,128)(2,1)} %refs_0_.1, bf16[4,2,4096]{2,1,0:T(2,128)(2,1)} %refs_1_.1, f32[2,64,64]{2,1,0:T(8,128)} %refs_2_.1, f32[2,64,64]{2,1,0:T(8,128)} %refs_3_.1, f32[2,64]{1,0:T(2,128)} %refs_4_.1, f32[2,64]{1,0:T(2,128)} %refs_5_.1), custom_call_target="tpu_custom_call" | custom-call | tf_op jit(solution)/shard_map/pallas_call | solution.py:213
  23.2 1.3 %copy.8 = f32[256,16]{0,1:T(8,128)} copy(f32[256,16]{0,1:T(8,128)} %bitcast.1) | data formatting | bytes 32768

commit v2 on v1

--- a/solution.py
+++ b/solution.py
@@ -7,6 +7,7 @@
 
 RA = 64
 RB = 64
+SIDES = 2
 MESH = pl.DeviceIdType.MESH
 F32 = jnp.float32
 BF16 = jnp.bfloat16
@@ -36,21 +37,23 @@
     chunks = qv.shape[0]
     q_rows = qv.shape[1]
     t_rows = tv.shape[1]
-    half = chunks // 2
-    last = n // 2
-
-    def block_at(pos):
-        pos = lax.rem(pos + 2 * n, n)
-        return jnp.where(pos < last, 2 * pos, 2 * (n - 1 - pos) + 1)
-
-    pos = jnp.where(lax.rem(me, 2) == 0, me // 2, n - 1 - me // 2)
-    right = (group, block_at(pos + 1), layer)
-    left = (group, block_at(pos - 1), layer)
+
+    line = n // 2
+    across_at = me + 1 - 2 * lax.rem(me, 2)
+    across = (group, across_at, layer)
+
+    def peer(i):
+        return (group, lax.rem(me + 2 * i, n), layer)
+
     partner = (group, me, 1 - layer)
 
     barrier = pltpu.get_barrier_semaphore()
-    for device in (right, left, partner):
+    for device in (partner, across):
         pl.semaphore_signal(barrier, inc=1, device_id=device, device_id_type=MESH)
+
+    @pl.loop(1, line)
+    def _(i):
+        pl.semaphore_signal(barrier, inc=1, device_id=peer(i), device_id_type=MESH)
 
     def t_copy(c):
         return pltpu.make_async_copy(
@@ -116,50 +119,51 @@
     mine = jnp.where(parity == 0, final[:, :128], final[:, 128:])
     blocks[me] = mine.reshape(chunks, step, 128).astype(BF16)
 
-    pl.semaphore_wait(barrier, 3)
-
-    def hop(flow, d, side):
-        owner = block_at(pos - d + 1 if flow == 0 else pos + d - 1)
-        piece = blocks.at[owner, pl.ds(side * half, half)]
+    pl.semaphore_wait(barrier, line + 1)
+
+    span = chunks // SIDES
+
+    def along(i, owner, side):
+        piece = blocks.at[owner, pl.ds(side * span, span)]
         return pltpu.make_async_remote_copy(
             src_ref=piece, dst_ref=piece,
-            send_sem=send_sem.at[flow, d - 1, side], recv_sem=recv_sem.at[flow, d - 1, side],
-            device_id=right if flow == 0 else left, device_id_type=MESH)
-
-    def arrival(flow, d, side):
-        owner = block_at(pos - d if flow == 0 else pos + d)
-        piece = blocks.at[owner, pl.ds(side * half, half)]
+            send_sem=send_sem.at[side, i], recv_sem=recv_sem.at[side, i],
+            device_id=peer(i), device_id_type=MESH)
+
+    def over(i, owner, side):
+        piece = blocks.at[owner, pl.ds(side * span, span)]
         return pltpu.make_async_remote_copy(
             src_ref=piece, dst_ref=piece,
-            send_sem=send_sem.at[flow, d - 1, side], recv_sem=recv_sem.at[flow, d - 1, side],
-            device_id=right if flow == 0 else left, device_id_type=MESH)
-
-    for side in range(2):
-        for flow in range(2):
-            hop(flow, 1, (side + flow) % 2).start()
-
-    @pl.loop(1, last - 1)
-    def _(d):
-        for side in range(2):
-            for flow in range(2):
-                arrival(flow, d, (side + flow) % 2).wait_recv()
-                hop(flow, d + 1, (side + flow) % 2).start()
-
-    for flow in range(2):
-        arrival(flow, last - 1, flow).wait_recv()
-        hop(flow, last, flow).start()
-    for flow in range(2):
-        arrival(flow, last - 1, 1 - flow).wait_recv()
+            send_sem=send_sem.at[side, line + i], recv_sem=recv_sem.at[side, line + i],
+            device_id=across, device_id_type=MESH)
+
+    def source(base, i):
+        return lax.rem(base + n - 2 * i, n)
+
+    for side in range(SIDES):
+        over(0, me, side).start()
+
+        @pl.loop(1, line)
+        def _(i):
+            along(i, me, side).start()
+
+    for side in range(SIDES):
+        @pl.loop(1, line)
+        def _(i):
+            along(i, source(me, i), side).wait_recv()
+            over(i, source(me, i), side).start()
 
     @pl.loop(0, chunks)
     def _(c):
         q_copy(c).wait()
-
-    for flow in range(2):
-        arrival(flow, last, flow).wait_recv()
 
     total = None
     for c in range(0, chunks, 2):
+        if c % span == 0:
+            @pl.loop(0, line)
+            def _(i):
+                over(i, source(across_at, i), c // span).wait_recv()
+
         lhs = jnp.concatenate([qv[c + i].reshape(2 * q_rows, 128) for i in range(2)], axis=1)
         rhs = jnp.concatenate(
             [blocks[:, c + i].astype(F32).reshape(n * step, 128).astype(BF16) for i in range(2)], axis=1)
@@ -187,13 +191,13 @@
         device_id=partner, device_id_type=MESH)
     swap.start()
 
-    @pl.loop(1, last)
-    def _(d):
-        for side in range(2):
-            for flow in range(2):
-                hop(flow, d, side).wait_send()
-    for flow in range(2):
-        hop(flow, last, flow).wait_send()
+    for side in range(SIDES):
+        over(0, me, side).wait_send()
+
+        @pl.loop(1, line)
+        def _(i):
+            along(i, me, side).wait_send()
+            over(i, source(me, i), side).wait_send()
     swap.wait()
     out_ref[...] = part[layer] + other[...]
 
@@ -227,8 +231,8 @@
                 pltpu.VMEM((keep, q_rows), F32),
                 pltpu.SemaphoreType.DMA((chunks,)),
                 pltpu.SemaphoreType.DMA((chunks,)),
-                pltpu.SemaphoreType.DMA((2, n // 2, 2)),
-                pltpu.SemaphoreType.DMA((2, n // 2, 2)),
+                pltpu.SemaphoreType.DMA((SIDES, n)),
+                pltpu.SemaphoreType.DMA((SIDES, n)),
                 pltpu.SemaphoreType.DMA,
                 pltpu.SemaphoreType.DMA,
             ],

time: 24.7 us -> 22.2 us (0.90)
  Pallas kernels: 23.2 us -> 20.6 us
    pallas_call x1, Pallas kernels: 23.2 us -> 20.6 us  [shards(): pl.pallas_call(lambda *refs: kernel(n, scale, *refs), out_shape=jax.Shape...]
where the time goes in v2:
time: 22.2 us; the launch traced here: 22 us
  Pallas kernels  20.6 us (93%)
  local copies, waits for them, and re-layouts  1.32 us (6%)
    pallas_call x1, Pallas kernels, shards(): pl.pallas_call(lambda *refs: kernel(n, scale, *refs), out_shape=jax.Shape...  20.6 us
    unnamed x1, local copies, waits for them, and re-layouts  1.32 us

profile of v2, /device:TPU:0, one launch (start us, length us, event | category | flops | bytes accessed | tf_op | source)
XLA Modules:
  0.0 22.0 jit_solution(5670664979979551241)
XLA Ops:
  0.0 20.6 %shard_map.64 = f32[16,256]{1,0:T(8,128)} custom-call(bf16[256,2,4096]{2,1,0:T(2,128)(2,1)} %refs_0_.1, bf16[4,2,4096]{2,1,0:T(2,128)(2,1)} %refs_1_.1, f32[2,64,64]{2,1,0:T(8,128)} %refs_2_.1, f32[2,64,64]{2,1,0:T(8,128)} %refs_3_.1, f32[2,64]{1,0:T(2,128)} %refs_4_.1, f32[2,64]{1,0:T(2,128)} %refs_5_.1), custom_call_target="tpu_custom_call" | custom-call | tf_op jit(solution)/shard_map/pallas_call | solution.py:217
  20.6 1.3 %copy.8 = f32[256,16]{0,1:T(8,128)} copy(f32[256,16]{0,1:T(8,128)} %bitcast.1) | data formatting | bytes 32768

commit v3 on v2

--- a/solution.py
+++ b/solution.py
@@ -66,10 +66,6 @@
     @pl.loop(0, chunks)
     def _(c):
         t_copy(c).start()
-
-    @pl.loop(0, chunks)
-    def _(c):
-        q_copy(c).start()
 
     b0, b1 = b_ref[0], b_ref[1]
     both = jnp.concatenate([b0, b1], axis=1)
@@ -146,6 +142,10 @@
         @pl.loop(1, line)
         def _(i):
             along(i, me, side).start()
+
+    @pl.loop(0, chunks)
+    def _(c):
+        q_copy(c).start()
 
     for side in range(SIDES):
         @pl.loop(1, line)

time: 22.2 us -> 22.2 us (level)
  no operation moved by 1% of the time
where the time goes in v3:
time: 22.2 us; the launch traced here: 22 us
  Pallas kernels  20.6 us (93%)
  local copies, waits for them, and re-layouts  1.32 us (6%)
    pallas_call x1, Pallas kernels, shards(): pl.pallas_call(lambda *refs: kernel(n, scale, *refs), out_shape=jax.Shape...  20.6 us
    unnamed x1, local copies, waits for them, and re-layouts  1.32 us

profile of v3, /device:TPU:0, one launch (start us, length us, event | category | flops | bytes accessed | tf_op | source)
XLA Modules:
  0.0 22.0 jit_solution(14148704502143540935)
XLA Ops:
  0.0 20.6 %shard_map.64 = f32[16,256]{1,0:T(8,128)} custom-call(bf16[256,2,4096]{2,1,0:T(2,128)(2,1)} %refs_0_.1, bf16[4,2,4096]{2,1,0:T(2,128)(2,1)} %refs_1_.1, f32[2,64,64]{2,1,0:T(8,128)} %refs_2_.1, f32[2,64,64]{2,1,0:T(8,128)} %refs_3_.1, f32[2,64]{1,0:T(2,128)} %refs_4_.1, f32[2,64]{1,0:T(2,128)} %refs_5_.1), custom_call_target="tpu_custom_call" | custom-call | tf_op jit(solution)/shard_map/pallas_call | solution.py:217
  20.6 1.3 %copy.8 = f32[256,16]{0,1:T(8,128)} copy(f32[256,16]{0,1:T(8,128)} %bitcast.1) | data formatting | bytes 32768

commit v4 on v3

--- a/solution.py
+++ b/solution.py
@@ -63,7 +63,7 @@
         return pltpu.make_async_copy(
             q_hbm.at[:, :, pl.ds(pl.multiple_of(c * 128, 128), 128)], qv.at[c], q_sem.at[c])
 
-    @pl.loop(0, chunks)
+    @pl.loop(0, chunks, unroll=8)
     def _(c):
         t_copy(c).start()
 
@@ -73,7 +73,7 @@
     right_mat = jnp.concatenate(
         [jnp.concatenate([both, zero], axis=1), jnp.concatenate([zero, both], axis=1)], axis=0)
 
-    @pl.loop(0, chunks)
+    @pl.loop(0, chunks, unroll=8)
     def _(c):
         t_copy(c).wait()
 

time: 22.2 us -> 22.2 us (level)
  no operation moved by 1% of the time
where the time goes in v4:
time: 22.2 us; the launch traced here: 21.9 us
  Pallas kernels  20.6 us (93%)
  local copies, waits for them, and re-layouts  1.32 us (6%)
    pallas_call x1, Pallas kernels, shards(): pl.pallas_call(lambda *refs: kernel(n, scale, *refs), out_shape=jax.Shape...  20.6 us
    unnamed x1, local copies, waits for them, and re-layouts  1.32 us

profile of v4, /device:TPU:0, one launch (start us, length us, event | category | flops | bytes accessed | tf_op | source)
XLA Modules:
  0.0 21.9 jit_solution(18137784860795531369)
XLA Ops:
  0.0 20.6 %shard_map.64 = f32[16,256]{1,0:T(8,128)} custom-call(bf16[256,2,4096]{2,1,0:T(2,128)(2,1)} %refs_0_.1, bf16[4,2,4096]{2,1,0:T(2,128)(2,1)} %refs_1_.1, f32[2,64,64]{2,1,0:T(8,128)} %refs_2_.1, f32[2,64,64]{2,1,0:T(8,128)} %refs_3_.1, f32[2,64]{1,0:T(2,128)} %refs_4_.1, f32[2,64]{1,0:T(2,128)} %refs_5_.1), custom_call_target="tpu_custom_call" | custom-call | tf_op jit(solution)/shard_map/pallas_call | solution.py:217
  20.6 1.3 %copy.8 = f32[256,16]{0,1:T(8,128)} copy(f32[256,16]{0,1:T(8,128)} %bitcast.1) | data formatting | bytes 32768
